TPU v7x, 512 devices: a whole 4x4x16 slice. The times are simulated.
512 devices in a mesh: grp: 8 (over y, core), dom: 64 (over x, z).
Axes of the slice: x: 4, y: 4, z: 16, core: 2. Of those that a mesh axis runs over, the one named last changes fastest.
Arguments:
- positions: float32 [16384, 3, 128], P(('grp', 'dom')), may hold values from 0 to 1
- masses: float32 [16384, 128], P(('grp', 'dom')), may hold values from 0.5 to 2
- velocities: float32 [16384, 3, 128], P(('grp', 'dom')), may hold values from -3 to 3
- dest_dom: int32 [16384], P(('grp', 'dom')), may hold values from 0 to 63, as said below
- local_pairs: int32 [16384, 4], P(('grp', 'dom')), may hold values from 0 to 31
- export_list: int32 [2560, 4], P(('grp', 'dom')), may hold values from 0 to 31
- cross_pairs: int32 [10240, 4], P(('grp', 'dom')), may hold values from 0 to 31
Outputs:
- positions_out: float32 [16384, 3, 128], P(('grp', 'dom'))
- velocities_out: float32 [16384, 3, 128], P(('grp', 'dom'))
Inputs may be any that keep to these rules, and one draw needn't show every extreme that they name: `dest_dom`: every device receives exactly 32 blocks; no device sends more than 2 blocks to one device, and in every group some device sends exactly 2 to one device. Inside a group every device sends equally many blocks to the device a given cyclic distance away along dom.
All inputs are finite; a program needn't handle non-finite values.
Results may differ from a plain program's by a relative error of at most 0.0003.
Values sent between devices are 32-bit elements; how exact they have to be, the bound alone decides.
A program may use at most 64 MiB of HBM per device.

v0:
```python
import math

import jax
import jax.numpy as jnp
from jax import lax
from jax.sharding import PartitionSpec as P

ROUNDS = 5
EXPORTS = 4
FAR = 4


GRAVITY = 0.01
SOFTENING = 0.05
SPLIT_SCALE = 0.3
TIMESTEP = 0.5


def from_partner(block, axis, distance):
    count = lax.axis_size(axis)
    route = []
    for low in range(count):
        high = low | 1 << distance
        if high != low and high < count:
            route += [(low, high), (high, low)]
    return lax.ppermute(block, axis, route)


def block_accel(target_pos, source_pos, source_mass):
    separation = source_pos[:, :, None, :] - target_pos[None, :, :, None]
    distance_sq = jnp.sum(separation * separation, axis=1)
    distance = jnp.sqrt(distance_sq)
    softened = distance_sq + SOFTENING * SOFTENING
    inverse = 1.0 / (softened * jnp.sqrt(softened))
    scaled = distance / (2.0 * SPLIT_SCALE)
    shaping = lax.erfc(scaled) + distance / (SPLIT_SCALE * math.sqrt(math.pi)) * jnp.exp(
        -scaled * scaled
    )
    weight = source_mass[:, None, :] * shaping * inverse
    return GRAVITY * jnp.sum(separation * weight[:, None, :, :], axis=(0, 3))


def local_accel(new_pos, new_mass, local_pairs):
    block_count = new_pos.shape[0]
    batch_width = 4
    groups = block_count // batch_width
    near_pos = new_pos[local_pairs]
    near_mass = new_mass[local_pairs]

    def batch_step(batch_items):
        return jax.vmap(block_accel)(batch_items[0], batch_items[1], batch_items[2])

    shaped = (
        new_pos.reshape((groups, batch_width) + new_pos.shape[1:]),
        near_pos.reshape((groups, batch_width) + near_pos.shape[1:]),
        near_mass.reshape((groups, batch_width) + near_mass.shape[1:]),
    )
    return lax.map(batch_step, shaped).reshape(new_pos.shape)


def on_device(positions, masses, velocities, dest_dom, local_pairs, export_list, cross_pairs):
    block_count = positions.shape[0]
    domain_count = lax.axis_size("dom")
    capacity = max(2, (2 * block_count + domain_count - 1) // domain_count)
    slot_count = domain_count * capacity
    peer_ids = jnp.arange(domain_count, dtype=jnp.int32)
    chosen = (dest_dom[:, None] == peer_ids[None, :]).astype(jnp.int32)
    earlier = jnp.sum((jnp.cumsum(chosen, axis=0) - chosen) * chosen, axis=1)
    send_slot = dest_dom * capacity + earlier

    def pack_slots(values):
        return jnp.zeros((slot_count,) + values.shape[1:], values.dtype).at[send_slot].set(values)

    filled = jnp.zeros((slot_count,), jnp.float32).at[send_slot].set(1.0)
    got_pos, got_mass, got_vel, got_fill = (
        lax.all_to_all(pack_slots(positions), "dom", split_axis=0, concat_axis=0, tiled=True),
        lax.all_to_all(pack_slots(masses), "dom", split_axis=0, concat_axis=0, tiled=True),
        lax.all_to_all(pack_slots(velocities), "dom", split_axis=0, concat_axis=0, tiled=True),
        lax.all_to_all(filled, "dom", split_axis=0, concat_axis=0, tiled=True),
    )
    arrival = jnp.where(got_fill > 0.5, jnp.cumsum(got_fill) - 1.0, 1.0 * block_count).astype(
        jnp.int32
    )

    def unpack_slots(values):
        return (
            jnp.zeros((block_count,) + values.shape[1:], values.dtype)
            .at[arrival]
            .set(values, mode="drop")
        )

    new_pos = unpack_slots(got_pos)
    new_mass = unpack_slots(got_mass)
    acceleration = local_accel(new_pos, new_mass, local_pairs)
    new_vel = unpack_slots(got_vel)
    device_count = lax.axis_size(("grp", "dom"))
    bit_count = device_count.bit_length() - 1
    crosses = cross_pairs.reshape(ROUNDS, EXPORTS, FAR)
    for phase_number in range(ROUNDS):
        bit_number = phase_number * bit_count // ROUNDS
        picked = export_list[phase_number]
        sources = crosses[phase_number]
        visiting = from_partner(new_pos[picked], ("grp", "dom"), bit_number)
        partial_acc = jax.vmap(block_accel)(visiting, new_pos[sources], new_mass[sources])
        returned = from_partner(partial_acc, ("grp", "dom"), bit_number)
        acceleration = acceleration.at[picked].add(returned)
    velocities_out = new_vel + TIMESTEP * acceleration
    positions_out = new_pos + TIMESTEP * velocities_out
    return (positions_out, velocities_out)


def solution(mesh):
    placed = (
        P(("grp", "dom"), None, None),
        P(("grp", "dom"), None),
        P(("grp", "dom"), None, None),
        P(("grp", "dom")),
        P(("grp", "dom"), None),
        P(("grp", "dom"), None),
        P(("grp", "dom"), None),
    )
    return jax.shard_map(
        on_device,
        mesh=mesh,
        in_specs=placed,
        out_specs=(P(("grp", "dom"), None, None), P(("grp", "dom"), None, None)),
        check_vma=False,
    )
```

profile of v0, /device:TPU:6, one launch (start us, length us, event | category | flops | bytes accessed | tf_op | source)
XLA Modules:
  0.0 217.4 jit_solution(13792425114290377953)
XLA Ops:
  4.4 18.8 %all-to-all-start = ((f32[64,2,1]{1,2,0:T(1,128)}), f32[64,2,1]{1,2,0:T(1,128)S(1)}, u32[]{:S(2)}, u32[]{:S(2)}) async-start(f32[64,2,1]{1,2,0:T(1,128)} %bitcast.4), calls=%async_computation | async-start | bytes 65536 | tf_op jit(solution)/shard_map/all_to_all | solution.py:79
  28.6 3.5 %scatter_fusion = f32[128,3,128]{2,1,0:T(4,128)} fusion(f32[128,3,128]{2,1,0:T(4,128)} %broadcast.1298.clone, s32[32]{0:T(128)S(1)} %compare_select_fusion.12, f32[32,3,128]{2,1,0:T(4,128)S(1)} %copy.58), kind=kCustom, calls=%fused_computation.18 | custom fusion | bytes 147584 | tf_op jit(solution)/shard_map/scatter | solution.py:72
  35.6 13.1 %all-to-all-start.1 = ((f32[128,3,128]{2,1,0:T(4,128)}), f32[128,3,128]{2,1,0:T(4,128)S(1)}, u32[]{:S(2)}, u32[]{:S(2)}) async-start(f32[128,3,128]{2,1,0:T(4,128)} %scatter_fusion), calls=%async_computation.1 | async-start | bytes 524288 | tf_op jit(solution)/shard_map/all_to_all | solution.py:76
  48.8 20.3 %all-to-all-done.1 = f32[128,3,128]{2,1,0:T(4,128)S(1)} async-done(((f32[128,3,128]{2,1,0:T(4,128)}), f32[128,3,128]{2,1,0:T(4,128)S(1)}, u32[]{:S(2)}, u32[]{:S(2)}) %all-to-all-start.1) | async-done | bytes 196640 | tf_op jit(solution)/shard_map/all_to_all | solution.py:76
  69.1 6.6 %all-to-all-start.3 = ((f32[64,2,128]{2,1,0:T(2,128)}), f32[64,2,128]{2,1,0:T(2,128)S(1)}, u32[]{:S(2)}, u32[]{:S(2)}) async-start(f32[64,2,128]{2,1,0:T(2,128)} %bitcast.7), calls=%async_computation.3 | async-start | bytes 131072 | tf_op jit(solution)/shard_map/all_to_all | solution.py:77
  77.4 4.6 %scatter_fusion.1 = f32[32,3,128]{2,1,0:T(4,128)S(1)} fusion(f32[32,3,128]{2,1,0:T(4,128)S(1)} %broadcast.1291.clone, s32[128]{0:T(128)S(1)} %fusion.90, f32[128,3,128]{2,1,0:T(4,128)S(1)} %all-to-all-done.1), kind=kCustom, calls=%fused_computation.19 | custom fusion | bytes 590336 | tf_op jit(solution)/shard_map/scatter | solution.py:89
  82.5 3.4 %collective-permute-start = (f32[4,3,128]{2,1,0:T(4,128)S(1)}, f32[4,3,128]{2,1,0:T(4,128)S(1)}, u32[]{:S(2)}, u32[]{:S(2)}) collective-permute-start(f32[4,3,128]{2,1,0:T(4,128)S(1)} %gather_fusion.3), channel_id=1, source_target_pairs={{0,1},{1,0},{2,3},{3,2},{4,5},{5,4},{6,7},{7,6},{8,9},{9,8},{10,11... | collective-permute-start | bytes 18440 | tf_op jit(solution)/shard_map/ppermute | solution.py:26
  86.7 3.5 %scatter_fusion.2 = f32[128,3,128]{2,1,0:T(4,128)} fusion(f32[128,3,128]{2,1,0:T(4,128)} %broadcast.1298.clone.1, s32[32]{0:T(128)S(1)} %compare_select_fusion.12, f32[32,3,128]{2,1,0:T(4,128)S(1)} %copy.59), kind=kCustom, calls=%fused_computation.20 | custom fusion | bytes 147584 | tf_op jit(solution)/shard_map/scatter | solution.py:72
  90.2 14.3 %all-to-all-start.2 = ((f32[128,3,128]{2,1,0:T(4,128)}), f32[128,3,128]{2,1,0:T(4,128)S(1)}, u32[]{:S(2)}, u32[]{:S(2)}) async-start(f32[128,3,128]{2,1,0:T(4,128)} %scatter_fusion.2), calls=%async_computation.2 | async-start | bytes 524288 | tf_op jit(solution)/shard_map/all_to_all | solution.py:78
  113.1 4.3 %collective-permute-start.2 = (f32[4,3,128]{2,1,0:T(4,128)S(1)}, f32[4,3,128]{2,1,0:T(4,128)S(1)}, u32[]{:S(2)}, u32[]{:S(2)}) collective-permute-start(f32[4,3,128]{2,1,0:T(4,128)S(1)} %gather_fusion.6), channel_id=1, source_target_pairs={{0,2},{2,0},{1,3},{3,1},{4,6},{6,4},{5,7},{7,5},{8,10},{10,8},{9,1... | collective-permute-start | bytes 18440 | tf_op jit(solution)/shard_map/ppermute | solution.py:26
  117.9 10.3 %collective-permute-start.4 = (f32[4,3,128]{2,1,0:T(4,128)S(1)}, f32[4,3,128]{2,1,0:T(4,128)S(1)}, u32[]{:S(2)}, u32[]{:S(2)}) collective-permute-start(f32[4,3,128]{2,1,0:T(4,128)S(1)} %gather_fusion.9), channel_id=1, source_target_pairs={{0,8},{8,0},{1,9},{9,1},{2,10},{10,2},{3,11},{11,3},{4,12},{12,4},... | collective-permute-start | bytes 18440 | tf_op jit(solution)/shard_map/ppermute | solution.py:26
  128.8 3.1 %collective-permute-start.6 = (f32[4,3,128]{2,1,0:T(4,128)S(1)}, f32[4,3,128]{2,1,0:T(4,128)S(1)}, u32[]{:S(2)}, u32[]{:S(2)}) collective-permute-start(f32[4,3,128]{2,1,0:T(4,128)S(1)} %gather_fusion.12), channel_id=1, source_target_pairs={{0,32},{32,0},{1,33},{33,1},{2,34},{34,2},{3,35},{35,3},{4,36},{36... | collective-permute-start | bytes 18440 | tf_op jit(solution)/shard_map/ppermute | solution.py:26
  132.6 3.5 %collective-permute-start.8 = (f32[4,3,128]{2,1,0:T(4,128)S(1)}, f32[4,3,128]{2,1,0:T(4,128)S(1)}, u32[]{:S(2)}, u32[]{:S(2)}) collective-permute-start(f32[4,3,128]{2,1,0:T(4,128)S(1)} %gather_fusion.15), channel_id=1, source_target_pairs={{0,128},{128,0},{1,129},{129,1},{2,130},{130,2},{3,131},{131,3},{4... | collective-permute-start | bytes 18440 | tf_op jit(solution)/shard_map/ppermute | solution.py:26
  143.3 3.1 %fusion.35 = f32[4,4,128,128]{3,2,1,0:T(8,128)S(1)} fusion(f32[4,4,128,128]{3,2,1,0:T(8,128)S(1)} %fusion.17, f32[4,4,128]{2,1,0:T(4,128)S(1)} %bitcast.73), kind=kLoop, calls=%fused_computation.101 | loop fusion | flops 18612224 | bytes 2105344 | tf_op jit(solution)/shard_map/vmap()/mul | solution.py:39
  147.1 4.3 %collective-permute-start.3 = (f32[4,3,128]{2,1,0:T(4,128)S(1)}, f32[4,3,128]{2,1,0:T(4,128)S(1)}, u32[]{:S(2)}, u32[]{:S(2)}) collective-permute-start(f32[4,3,128]{2,1,0:T(4,128)S(1)} %broadcast_multiply_fusion.3), channel_id=1, source_target_pairs={{0,2},{2,0},{1,3},{3,1},{4,6},{6,4},{5,7},{7,5},{8,10},{10,8},{9,1... | collective-permute-start | bytes 18440 | tf_op jit(solution)/shard_map/ppermute | solution.py:26
  155.5 3.3 %collective-permute-start.5 = (f32[4,3,128]{2,1,0:T(4,128)S(1)}, f32[4,3,128]{2,1,0:T(4,128)S(1)}, u32[]{:S(2)}, u32[]{:S(2)}) collective-permute-start(f32[4,3,128]{2,1,0:T(4,128)S(1)} %broadcast_multiply_fusion.2), channel_id=1, source_target_pairs={{0,8},{8,0},{1,9},{9,1},{2,10},{10,2},{3,11},{11,3},{4,12},{12,4},... | collective-permute-start | bytes 18440 | tf_op jit(solution)/shard_map/ppermute | solution.py:26
  163.1 4.2 %collective-permute-start.7 = (f32[4,3,128]{2,1,0:T(4,128)S(1)}, f32[4,3,128]{2,1,0:T(4,128)S(1)}, u32[]{:S(2)}, u32[]{:S(2)}) collective-permute-start(f32[4,3,128]{2,1,0:T(4,128)S(1)} %broadcast_multiply_fusion.1), channel_id=1, source_target_pairs={{0,32},{32,0},{1,33},{33,1},{2,34},{34,2},{3,35},{35,3},{4,36},{36... | collective-permute-start | bytes 18440 | tf_op jit(solution)/shard_map/ppermute | solution.py:26
  167.7 3.1 %fusion.56 = f32[4,4,128,128]{3,2,1,0:T(8,128)S(1)} fusion(f32[4,4,128,128]{3,2,1,0:T(8,128)S(1)} %fusion.23, f32[4,4,128]{2,1,0:T(4,128)S(1)} %bitcast.70), kind=kLoop, calls=%fused_computation.122 | loop fusion | flops 18612224 | bytes 2105344 | tf_op jit(solution)/shard_map/vmap()/mul | solution.py:39
  174.1 34.1 %while.10 = (s32[]{:T(128)}, f32[8,4,3,128]{3,2,1,0:T(4,128)S(1)}, f32[8,4,4,3,128]{4,3,2,1,0:T(4,128)S(1)}, f32[8,4,3,128]{3,2,1,0:T(4,128)S(1)}, f32[8,4,4,128]{3,2,1,0:T(4,128)S(1)}, /*index=5*/s32[]{:T(128)}) while((s32[]{:T(128)}, f32[8,4,3,128]{3,2,1,0:T(4,128)S(1)}, f32[8,4,4,3,128]{4,3,2,1,0:T(4,128)S(1)}, ...), condition=%wide.region_13.14_spmd, body=%wide.region_10.13_spmd.sunk | while | flops 23068672 | bytes 4364373 | solution.py:58
  178.8 3.1 %fusion.107 = f32[4,4,128,128]{3,2,1,0:T(8,128)S(1)} fusion(f32[4,4,128,128]{3,2,1,0:T(8,128)S(1)} %fusion.106, f32[4,4,128]{2,1,0:T(4,128)S(1)} %dynamic-slice_bitcast_fusion.8), kind=kLoop, calls=%fused_computation.39.clone.1 | loop fusion | flops 18612224 | bytes 2105344 | tf_op jit(solution)/shard_map/while/body/eval_jaxpr/vmap()/mul | solution.py:39
  183.1 3.1 %fusion.107 = f32[4,4,128,128]{3,2,1,0:T(8,128)S(1)} fusion(f32[4,4,128,128]{3,2,1,0:T(8,128)S(1)} %fusion.106, f32[4,4,128]{2,1,0:T(4,128)S(1)} %dynamic-slice_bitcast_fusion.8), kind=kLoop, calls=%fused_computation.39.clone.1 | loop fusion | flops 18612224 | bytes 2105344 | tf_op jit(solution)/shard_map/while/body/eval_jaxpr/vmap()/mul | solution.py:39
  191.6 3.1 %fusion.107 = f32[4,4,128,128]{3,2,1,0:T(8,128)S(1)} fusion(f32[4,4,128,128]{3,2,1,0:T(8,128)S(1)} %fusion.106, f32[4,4,128]{2,1,0:T(4,128)S(1)} %dynamic-slice_bitcast_fusion.8), kind=kLoop, calls=%fused_computation.39.clone.1 | loop fusion | flops 18612224 | bytes 2105344 | tf_op jit(solution)/shard_map/while/body/eval_jaxpr/vmap()/mul | solution.py:39
  195.8 3.1 %fusion.107 = f32[4,4,128,128]{3,2,1,0:T(8,128)S(1)} fusion(f32[4,4,128,128]{3,2,1,0:T(8,128)S(1)} %fusion.106, f32[4,4,128]{2,1,0:T(4,128)S(1)} %dynamic-slice_bitcast_fusion.8), kind=kLoop, calls=%fused_computation.39.clone.1 | loop fusion | flops 18612224 | bytes 2105344 | tf_op jit(solution)/shard_map/while/body/eval_jaxpr/vmap()/mul | solution.py:39
  208.2 4.6 %scatter_fusion.3 = f32[32,3,128]{2,1,0:T(4,128)S(1)} fusion(f32[32,3,128]{2,1,0:T(4,128)S(1)} %broadcast.1291.clone.1, s32[128]{0:T(128)S(1)} %fusion.90, f32[128,3,128]{2,1,0:T(4,128)S(1)} %all-to-all-done.2), kind=kCustom, calls=%fused_computation.21 | custom fusion | bytes 590336 | tf_op jit(solution)/shard_map/scatter | solution.py:89
  (164 shorter events, 71.7 us)
Async XLA Ops:
  4.4 31.3 %all-to-all-start = ((f32[64,2,1]{1,2,0:T(1,128)}), f32[64,2,1]{1,2,0:T(1,128)S(1)}, u32[]{:S(2)}, u32[]{:S(2)}) async-start(f32[64,2,1]{1,2,0:T(1,128)} %bitcast.4), calls=%async_computation | async-start | bytes 65536 | tf_op jit(solution)/shard_map/all_to_all | solution.py:79
  32.2 53.8 %copy-start = (f32[32,3,128]{2,0,1:T(8,128)S(1)}, f32[32,3,128]{2,0,1:T(8,128)}, u32[]{:S(2)}) copy-start(f32[32,3,128]{2,0,1:T(8,128)} %param.11) | copy-start | bytes 147460
  35.6 33.5 %all-to-all-start.1 = ((f32[128,3,128]{2,1,0:T(4,128)}), f32[128,3,128]{2,1,0:T(4,128)S(1)}, u32[]{:S(2)}, u32[]{:S(2)}) async-start(f32[128,3,128]{2,1,0:T(4,128)} %scatter_fusion), calls=%async_computation.1 | async-start | bytes 524288 | tf_op jit(solution)/shard_map/all_to_all | solution.py:76
  69.1 21.1 %all-to-all-start.3 = ((f32[64,2,128]{2,1,0:T(2,128)}), f32[64,2,128]{2,1,0:T(2,128)S(1)}, u32[]{:S(2)}, u32[]{:S(2)}) async-start(f32[64,2,128]{2,1,0:T(2,128)} %bitcast.7), calls=%async_computation.3 | async-start | bytes 131072 | tf_op jit(solution)/shard_map/all_to_all | solution.py:77
  82.5 53.5 %collective-permute-start = (f32[4,3,128]{2,1,0:T(4,128)S(1)}, f32[4,3,128]{2,1,0:T(4,128)S(1)}, u32[]{:S(2)}, u32[]{:S(2)}) collective-permute-start(f32[4,3,128]{2,1,0:T(4,128)S(1)} %gather_fusion.3), channel_id=1, source_target_pairs={{0,1},{1,0},{2,3},{3,2},{4,5},{5,4},{6,7},{7,6},{8,9},{9,8},{10,11... | collective-permute-start | bytes 18440 | tf_op jit(solution)/shard_map/ppermute | solution.py:26
  90.2 117.9 %all-to-all-start.2 = ((f32[128,3,128]{2,1,0:T(4,128)}), f32[128,3,128]{2,1,0:T(4,128)S(1)}, u32[]{:S(2)}, u32[]{:S(2)}) async-start(f32[128,3,128]{2,1,0:T(4,128)} %scatter_fusion.2), calls=%async_computation.2 | async-start | bytes 524288 | tf_op jit(solution)/shard_map/all_to_all | solution.py:78
  113.1 29.8 %collective-permute-start.2 = (f32[4,3,128]{2,1,0:T(4,128)S(1)}, f32[4,3,128]{2,1,0:T(4,128)S(1)}, u32[]{:S(2)}, u32[]{:S(2)}) collective-permute-start(f32[4,3,128]{2,1,0:T(4,128)S(1)} %gather_fusion.6), channel_id=1, source_target_pairs={{0,2},{2,0},{1,3},{3,1},{4,6},{6,4},{5,7},{7,5},{8,10},{10,8},{9,1... | collective-permute-start | bytes 18440 | tf_op jit(solution)/shard_map/ppermute | solution.py:26
  117.9 33.4 %collective-permute-start.4 = (f32[4,3,128]{2,1,0:T(4,128)S(1)}, f32[4,3,128]{2,1,0:T(4,128)S(1)}, u32[]{:S(2)}, u32[]{:S(2)}) collective-permute-start(f32[4,3,128]{2,1,0:T(4,128)S(1)} %gather_fusion.9), channel_id=1, source_target_pairs={{0,8},{8,0},{1,9},{9,1},{2,10},{10,2},{3,11},{11,3},{4,12},{12,4},... | collective-permute-start | bytes 18440 | tf_op jit(solution)/shard_map/ppermute | solution.py:26
  128.8 30.0 %collective-permute-start.6 = (f32[4,3,128]{2,1,0:T(4,128)S(1)}, f32[4,3,128]{2,1,0:T(4,128)S(1)}, u32[]{:S(2)}, u32[]{:S(2)}) collective-permute-start(f32[4,3,128]{2,1,0:T(4,128)S(1)} %gather_fusion.12), channel_id=1, source_target_pairs={{0,32},{32,0},{1,33},{33,1},{2,34},{34,2},{3,35},{35,3},{4,36},{36... | collective-permute-start | bytes 18440 | tf_op jit(solution)/shard_map/ppermute | solution.py:26
  132.6 34.7 %collective-permute-start.8 = (f32[4,3,128]{2,1,0:T(4,128)S(1)}, f32[4,3,128]{2,1,0:T(4,128)S(1)}, u32[]{:S(2)}, u32[]{:S(2)}) collective-permute-start(f32[4,3,128]{2,1,0:T(4,128)S(1)} %gather_fusion.15), channel_id=1, source_target_pairs={{0,128},{128,0},{1,129},{129,1},{2,130},{130,2},{3,131},{131,3},{4... | collective-permute-start | bytes 18440 | tf_op jit(solution)/shard_map/ppermute | solution.py:26
  140.2 72.5 %collective-permute-start.1 = (f32[4,3,128]{2,1,0:T(4,128)S(1)}, f32[4,3,128]{2,1,0:T(4,128)S(1)}, u32[]{:S(2)}, u32[]{:S(2)}) collective-permute-start(f32[4,3,128]{2,1,0:T(4,128)S(1)} %broadcast_multiply_fusion.4), channel_id=1, source_target_pairs={{0,1},{1,0},{2,3},{3,2},{4,5},{5,4},{6,7},{7,6},{8,9},{9,8},{10,11... | collective-permute-start | bytes 18440 | tf_op jit(solution)/shard_map/ppermute | solution.py:26
  147.1 66.3 %collective-permute-start.3 = (f32[4,3,128]{2,1,0:T(4,128)S(1)}, f32[4,3,128]{2,1,0:T(4,128)S(1)}, u32[]{:S(2)}, u32[]{:S(2)}) collective-permute-start(f32[4,3,128]{2,1,0:T(4,128)S(1)} %broadcast_multiply_fusion.3), channel_id=1, source_target_pairs={{0,2},{2,0},{1,3},{3,1},{4,6},{6,4},{5,7},{7,5},{8,10},{10,8},{9,1... | collective-permute-start | bytes 18440 | tf_op jit(solution)/shard_map/ppermute | solution.py:26
  155.5 58.6 %collective-permute-start.5 = (f32[4,3,128]{2,1,0:T(4,128)S(1)}, f32[4,3,128]{2,1,0:T(4,128)S(1)}, u32[]{:S(2)}, u32[]{:S(2)}) collective-permute-start(f32[4,3,128]{2,1,0:T(4,128)S(1)} %broadcast_multiply_fusion.2), channel_id=1, source_target_pairs={{0,8},{8,0},{1,9},{9,1},{2,10},{10,2},{3,11},{11,3},{4,12},{12,4},... | collective-permute-start | bytes 18440 | tf_op jit(solution)/shard_map/ppermute | solution.py:26
  163.1 51.7 %collective-permute-start.7 = (f32[4,3,128]{2,1,0:T(4,128)S(1)}, f32[4,3,128]{2,1,0:T(4,128)S(1)}, u32[]{:S(2)}, u32[]{:S(2)}) collective-permute-start(f32[4,3,128]{2,1,0:T(4,128)S(1)} %broadcast_multiply_fusion.1), channel_id=1, source_target_pairs={{0,32},{32,0},{1,33},{33,1},{2,34},{34,2},{3,35},{35,3},{4,36},{36... | collective-permute-start | bytes 18440 | tf_op jit(solution)/shard_map/ppermute | solution.py:26
  171.4 44.0 %collective-permute-start.9 = (f32[4,3,128]{2,1,0:T(4,128)S(1)}, f32[4,3,128]{2,1,0:T(4,128)S(1)}, u32[]{:S(2)}, u32[]{:S(2)}) collective-permute-start(f32[4,3,128]{2,1,0:T(4,128)S(1)} %broadcast_multiply_fusion), channel_id=1, source_target_pairs={{0,128},{128,0},{1,129},{129,1},{2,130},{130,2},{3,131},{131,3},{4... | collective-permute-start | bytes 18440 | tf_op jit(solution)/shard_map/ppermute | solution.py:26
where the time goes:
time: 218 us; the launch traced here: 217 us
  starting transfers between devices  94.4 us (43%)
  other arithmetic  62.4 us (29%)
  local copies, waits for them, and re-layouts  36.6 us (17%)
  waiting for transfers between devices  22.3 us (10%)
    ppermute x10, starting transfers between devices, from_partner(): return lax.ppermute(block, axis, route)  41.6 us
    mul x13, other arithmetic, block_accel(): weight = source_mass[:, None, :] * shaping * inverse  39.9 us
    all_to_all x1, waiting for transfers between devices, on_device(): lax.all_to_all(pack_slots(positions), 'dom', split_axis=0, concat_axis=0,...  20.3 us
    all_to_all x1, starting transfers between devices, on_device(): lax.all_to_all(filled, 'dom', split_axis=0, concat_axis=0, tiled=True)  18.8 us
    all_to_all x1, starting transfers between devices, on_device(): lax.all_to_all(pack_slots(velocities), 'dom', split_axis=0, concat_axis=0...  14.3 us
    all_to_all x1, starting transfers between devices, on_device(): lax.all_to_all(pack_slots(positions), 'dom', split_axis=0, concat_axis=0,...  13.1 us
    scatter x3, local copies, waits for them, and re-layouts, unpack_slots(): return jnp.zeros((block_count,) + values.shape[1:], values.dtype).at[arri...  10 us
    reduce_sum x13, other arithmetic, block_accel(): return GRAVITY * jnp.sum(separation * weight[:, None, :, :], axis=(0, 3))  8.82 us
  transfers between devices with their start and end apart: 14, of which 2 were waited for; matrix products, arithmetic and copies ran while one was open for 43% of the time, Pallas kernels for 0%

commit v1 on v0

v1 whole, which is shorter than its diff:
```python
import functools
import math

import jax
import jax.numpy as jnp
from jax import lax
from jax.experimental import pallas as pl
from jax.experimental.pallas import tpu as pltpu
from jax.sharding import PartitionSpec as P

BLOCK = 128
SLOTS = 32
NEAR = 4
ROUNDS = 5
EXPORTS = 4
FAR = 4
TIMESTEP = 0.5
F32, BF16 = jnp.float32, jnp.bfloat16
MESH = pl.DeviceIdType.MESH

ALPHA = math.log2(math.e) / 0.36
SOFT = ALPHA * 0.05**2
N0, N1, N2, N3 = 8.53126995, 11.49321071, 11.59229692, 5.3254959
D0, D1, D2 = 8.01883474, 10.80288261, 5.33752372
LEAD = 0.9399344975074229
SCALE = 0.01 * ALPHA**1.5 * LEAD
KEEP = 48
LATE = 12


def split3(x):
    first = x.astype(BF16).astype(F32)
    rest = x - first
    second = rest.astype(BF16).astype(F32)
    return first, second, rest - second


def exact_dot(choice, values):
    total = None
    for piece in split3(values):
        part = jnp.dot(choice, piece.astype(BF16), preferred_element_type=F32)
        total = part if total is None else total + part
    return total


def weight(raw):
    v = jnp.maximum(raw, 1e-30)
    u = v * lax.rsqrt(v)
    t = v + SOFT
    upper = (((u + N3) * u + N2) * u + N1) * u + N0
    lower = ((u + D2) * u + D1) * u + D0
    p = t * lower * jnp.exp2(v)
    return upper * lax.rsqrt(p * p * t)


def target_rows(x):
    row = lax.broadcasted_iota(jnp.int32, (8, BLOCK), 0)
    x = jnp.where(row < 3, x - 0.5, 0.0)
    norm = ALPHA * jnp.sum(x * x, axis=0, keepdims=True)
    own = jnp.where(row < 3, x, jnp.where(row == 3, norm, jnp.where(row == 4, 1.0, 0.0)))
    t1, t2, t3 = split3(own)
    return jnp.concatenate([t1, t2, t1, t2, t3, t1], axis=0).astype(BF16)


def source_rows(x):
    row = lax.broadcasted_iota(jnp.int32, (8, BLOCK), 0)
    mass = x[3:4]
    x = jnp.where(row < 3, x - 0.5, 0.0)
    norm = ALPHA * jnp.sum(x * x, axis=0, keepdims=True)
    own = jnp.where(row < 3, (-2.0 * ALPHA) * x, jnp.where(row == 3, 1.0, jnp.where(row == 4, norm, 0.0)))
    s1, s2, s3 = split3(own)
    moment = (SCALE * mass) * jnp.where(row < 3, x, jnp.where(row == 3, 1.0, 0.0))
    m1, m2, m3 = split3(moment)
    return (
        jnp.concatenate([s1, s1, s2, s2, s1, s3], axis=0),
        jnp.concatenate([m1, m2, m3, jnp.zeros_like(m1)], axis=0).astype(BF16),
    )


def pair_sum(x, features, source_ids, src, mom):
    highs, lows, moments = [], [], []
    for s in source_ids:
        raw = jnp.dot(src[s][:, :KEEP], features, preferred_element_type=F32)
        w = weight(raw)
        high = w.astype(BF16)
        highs.append(high)
        lows.append((w - high.astype(F32)).astype(BF16))
        moments.append(mom[s])
    moments = jnp.concatenate(moments, axis=1)
    a = jnp.dot(moments, jnp.concatenate(highs, axis=0), preferred_element_type=F32)
    a = a + jnp.dot(moments, jnp.concatenate(lows, axis=0), preferred_element_type=F32)
    a = a[0:8] + a[8:16] + a[16:24]
    return a - (x - 0.5) * a[3:4]


def flipped(index, bit):
    low = 2**bit
    return index + low * (1 - 2 * lax.rem(lax.div(index, low), 2))


def kernel(
    domains, bits, pos, mass, vel, dest, near_ids, export_ids, far_ids, pos_out, vel_out,
    pack_p, land_p, pack_v, land_v, new, tgt, src, mom, acc, out_x, in_x, out_a, in_a,
    move_send, move_recv, x_send, x_recv, a_send, a_recv,
):
    grp, dom = lax.axis_index("grp"), lax.axis_index("dom")
    inner = domains.bit_length() - 1

    def partner(bit):
        return (grp, flipped(dom, bit)) if bit < inner else (flipped(grp, bit - inner), dom)

    def peer(step):
        return (grp, lax.rem(dom + step, domains))

    barrier = pltpu.get_barrier_semaphore()
    outer = [bit for bit in bits if bit >= inner]

    @pl.loop(1, domains)
    def _(step):
        pl.semaphore_signal(barrier, inc=1, device_id=peer(step), device_id_type=MESH)

    for bit in outer:
        pl.semaphore_signal(barrier, inc=1, device_id=partner(bit), device_id_type=MESH)

    lane = lax.broadcasted_iota(jnp.int32, (1, BLOCK), 1)
    owner = lax.rem(lane, SLOTS)
    target = jnp.zeros((1, BLOCK), jnp.int32)
    for b in range(SLOTS):
        target = jnp.where(owner == b, dest[b], target)
    rows = lax.broadcasted_iota(jnp.int32, (SLOTS, BLOCK), 0)
    lanes = lax.broadcasted_iota(jnp.int32, (SLOTS, BLOCK), 1)
    owners = lax.rem(lanes, SLOTS)

    def as_column(row):
        return jnp.sum(jnp.where(lanes == rows, row, 0.0), axis=1, keepdims=True)

    target_f = target.astype(F32)
    same = (as_column(target_f) == target_f) & (rows < owners)
    rank = jnp.sum(jnp.where(same, 1.0, 0.0), axis=0, keepdims=True)
    away = lax.rem(target - dom + domains, domains)
    away_f = away.astype(F32)
    base = away_f * 8.0 + rank * 4.0
    came_from = lax.rem(dom - away + domains, domains).astype(F32) * 2.0 + rank
    place = jnp.sum(jnp.where(as_column(came_from) < came_from, 1.0, 0.0), axis=0, keepdims=True)

    def packed(stacked):
        key = base + lax.div(lane, SLOTS).astype(F32)
        count = lax.broadcasted_iota(jnp.int32, (domains * 8, BLOCK), 0).astype(F32)
        choice = jnp.where(count == key, 1.0, 0.0).astype(BF16)
        return exact_dot(choice, stacked).reshape(domains, 8, BLOCK)

    row8 = lax.broadcasted_iota(jnp.int32, (SLOTS * 8, BLOCK), 0)
    lane8 = lax.broadcasted_iota(jnp.int32, (SLOTS * 8, BLOCK), 1)
    found = (lane8 < SLOTS) & (place == lax.div(row8, 8).astype(F32))
    key = jnp.sum(jnp.where(found, base, 0.0), axis=1, keepdims=True)
    part = lax.rem(lax.broadcasted_iota(jnp.int32, (SLOTS * 8, 1), 0), 8)
    key = jnp.where(part < 4, key + part.astype(F32), -1.0)

    def unpacked(land):
        count = lax.broadcasted_iota(jnp.int32, (SLOTS * 8, domains * 8), 1).astype(F32)
        choice = jnp.where(count == key, 1.0, 0.0).astype(BF16)
        return exact_dot(choice, land.reshape(domains * 8, BLOCK)).reshape(SLOTS, 8, BLOCK)

    pack_p[...] = packed(jnp.concatenate([pos[:, 0], pos[:, 1], pos[:, 2], mass[...]], axis=0))
    pack_v[...] = packed(
        jnp.concatenate([vel[:, 0], vel[:, 1], vel[:, 2], jnp.zeros((SLOTS, BLOCK), F32)], axis=0)
    )
    pl.semaphore_wait(barrier, domains - 1 + len(outer))

    def move(pack, land, k):
        @pl.loop(1, domains)
        def _(step):
            pltpu.make_async_remote_copy(
                src_ref=pack.at[step], dst_ref=land.at[step],
                send_sem=move_send.at[k], recv_sem=move_recv.at[k],
                device_id=peer(step), device_id_type=MESH,
            ).start()

    def moved(pack, land, k):
        return pltpu.make_async_remote_copy(
            src_ref=pack.at[pl.ds(1, domains - 1)], dst_ref=land.at[pl.ds(1, domains - 1)],
            send_sem=move_send.at[k], recv_sem=move_recv.at[k],
            device_id=peer(1), device_id_type=MESH,
        )

    move(pack_p, land_p, 0)
    move(pack_v, land_v, 1)
    land_p[0] = pack_p[0]
    land_v[0] = pack_v[0]
    moved(pack_p, land_p, 0).wait_recv()
    new[...] = unpacked(land_p[...])

    def visit(r):
        return pltpu.make_async_remote_copy(
            src_ref=out_x.at[r], dst_ref=in_x.at[r], send_sem=x_send.at[r], recv_sem=x_recv.at[r],
            device_id=partner(bits[r]), device_id_type=MESH,
        )

    def give_back(r):
        return pltpu.make_async_remote_copy(
            src_ref=out_a.at[r], dst_ref=in_a.at[r], send_sem=a_send.at[r], recv_sem=a_recv.at[r],
            device_id=partner(bits[r]), device_id_type=MESH,
        )

    for r in range(ROUNDS):
        for e in range(EXPORTS):
            out_x[r, e] = new[export_ids[r, e]]
        visit(r).start()

    def prepare(b, carry):
        x = new[b]
        tgt[b] = target_rows(x)
        features, moments = source_rows(x)
        src[b] = jnp.concatenate([features, jnp.zeros((BLOCK - KEEP, BLOCK), F32)], axis=0).T.astype(BF16)
        mom[b] = moments
        return carry

    lax.fori_loop(0, SLOTS, prepare, 0, unroll=4)

    def near(b, carry):
        acc[b] = pair_sum(new[b], tgt[b], [near_ids[b, k] for k in range(NEAR)], src, mom)
        return carry

    lax.fori_loop(0, SLOTS - LATE, near, 0, unroll=4)
    for r in range(ROUNDS):
        visit(r).wait_recv()

        def far(e, carry, r=r):
            x = in_x[r, e]
            ids = [far_ids[r * EXPORTS + e, k] for k in range(FAR)]
            out_a[r, e] = pair_sum(x, target_rows(x), ids, src, mom)
            return carry

        lax.fori_loop(0, EXPORTS, far, 0, unroll=4)
        give_back(r).start()
    lax.fori_loop(SLOTS - LATE, SLOTS, near, 0, unroll=4)

    moved(pack_v, land_v, 1).wait_recv()
    new_vel = unpacked(land_v[...])
    wide = lax.broadcasted_iota(jnp.int32, (1, 256), 1)
    slot = jnp.full((1, 256), -1, jnp.int32)
    for r in range(ROUNDS):
        give_back(r).wait_recv()
        for e in range(EXPORTS):
            slot = jnp.where(lax.div(wide, 8) == r * EXPORTS + e, export_ids[r, e], slot)
    rows8 = lax.broadcasted_iota(jnp.int32, (SLOTS * 8, 256), 0)
    wide8 = lax.broadcasted_iota(jnp.int32, (SLOTS * 8, 256), 1)
    hit = (lax.div(rows8, 8) == slot) & (lax.rem(rows8, 8) == lax.rem(wide8, 8))
    returned = jnp.concatenate(
        [in_a[...].reshape(ROUNDS * EXPORTS * 8, BLOCK), jnp.zeros((256 - ROUNDS * EXPORTS * 8, BLOCK), F32)], axis=0
    )
    far_acc = exact_dot(jnp.where(hit, 1.0, 0.0).astype(BF16), returned).reshape(SLOTS, 8, BLOCK)
    new_vel = new_vel + TIMESTEP * (acc[...] + far_acc)
    new_pos = new[...] + TIMESTEP * new_vel
    pos_out[...] = new_pos[:, :3]
    vel_out[...] = new_vel[:, :3]
    for r in range(ROUNDS):
        visit(r).wait_send()
        give_back(r).wait_send()
    moved(pack_p, land_p, 0).wait_send()
    moved(pack_v, land_v, 1).wait_send()


def on_device(positions, masses, velocities, dest_dom, local_pairs, export_list, cross_pairs):
    domains = lax.axis_size("dom")
    devices = domains * lax.axis_size("grp")
    levels = devices.bit_length() - 1
    bits = [r * levels // ROUNDS for r in range(ROUNDS)]
    vmem, smem = pl.BlockSpec(memory_space=pltpu.VMEM), pl.BlockSpec(memory_space=pltpu.SMEM)
    moves = pltpu.VMEM((domains, 8, BLOCK), F32)
    visits = pltpu.VMEM((ROUNDS, EXPORTS, 8, BLOCK), F32)
    return pl.pallas_call(
        functools.partial(kernel, domains, bits),
        out_shape=(
            jax.ShapeDtypeStruct(positions.shape, F32),
            jax.ShapeDtypeStruct(velocities.shape, F32),
        ),
        in_specs=[vmem] * 3 + [smem] * 4,
        out_specs=(vmem, vmem),
        scratch_shapes=[
            moves, moves, moves, moves,
            pltpu.VMEM((SLOTS, 8, BLOCK), F32),
            pltpu.VMEM((SLOTS, KEEP, BLOCK), BF16),
            pltpu.VMEM((SLOTS, BLOCK, BLOCK), BF16),
            pltpu.VMEM((SLOTS, 32, BLOCK), BF16),
            pltpu.VMEM((SLOTS, 8, BLOCK), F32),
            visits, visits, visits, visits,
            pltpu.SemaphoreType.DMA((2,)), pltpu.SemaphoreType.DMA((2,)),
            pltpu.SemaphoreType.DMA((ROUNDS,)), pltpu.SemaphoreType.DMA((ROUNDS,)),
            pltpu.SemaphoreType.DMA((ROUNDS,)), pltpu.SemaphoreType.DMA((ROUNDS,)),
        ],
        compiler_params=pltpu.CompilerParams(
            collective_id=0, has_side_effects=True, vmem_limit_bytes=40 * 2**20
        ),
    )(positions, masses, velocities, dest_dom, local_pairs, export_list, cross_pairs)


def solution(mesh):
    both = ("grp", "dom")
    return jax.shard_map(
        on_device,
        mesh=mesh,
        in_specs=(
            P(both, None, None), P(both, None), P(both, None, None), P(both), P(both, None), P(both, None), P(both, None),
        ),
        out_specs=(P(both, None, None), P(both, None, None)),
        check_vma=False,
    )
```

time: 218 us -> 63.3 us (0.29)
  the two profiles are of different devices: /device:TPU:6 before, /device:TPU:8 now
where the time goes in v1:
time: 63.3 us; the launch traced here: 63 us
  Pallas kernels  58 us (92%)
  local copies, waits for them, and re-layouts  4.34 us (7%)
  between operations  0.68 us (1%)
    pallas_call x1, Pallas kernels, on_device(): pl.pallas_call(functools.partial(kernel, domains, bits), out_shape=(jax.S...  58 us
    unnamed x15, local copies, waits for them, and re-layouts  3.09 us

profile of v1, /device:TPU:8, one launch (start us, length us, event | category | flops | bytes accessed | tf_op | source)
XLA Modules:
  0.0 63.0 jit_solution(14553248593888996194)
XLA Ops:
  0.6 0.0 copy-start.3
  0.6 0.8 %copy.12.export_ids = s32[5,4]{1,0:T(8,128)S(1)} copy(s32[5,4]{0,1:T(4,128)} %param.12) | data formatting | bytes 160 | tf_op args[5]
  1.4 0.0 copy-done.3
  1.4 0.0 copy-start.4
  1.4 0.1 copy.13.far_ids
  1.5 0.6 copy-done.4
  2.1 0.1 copy.11.near_ids
  2.2 0.0 copy-start.2
  2.2 0.8 %copy.9.pos = f32[32,3,128]{2,1,0:T(4,128)S(1)} copy(f32[32,3,128]{2,0,1:T(8,128)} %param.7) | data formatting | bytes 98304 | tf_op args[0]
  3.0 0.0 copy-done.2
  3.0 0.0 copy-start
  3.1 0.0 copy-start.1
  3.1 0.7 %copy-done = f32[32,128]{1,0:T(8,128)S(1)} copy-done((f32[32,128]{1,0:T(8,128)S(1)}, f32[32,128]{1,0:T(8,128)}, u32[]{:S(2)}) %copy-start) | copy-done | bytes 16408
  3.8 0.0 copy-done.1
  3.8 58.0 %shard_map.86 = (f32[32,3,128]{2,1,0:T(4,128)S(1)}, f32[32,3,128]{2,1,0:T(4,128)S(1)}) custom-call(f32[32,3,128]{2,1,0:T(4,128)S(1)} %copy.9.pos, f32[32,128]{1,0:T(8,128)S(1)} %copy-done, f32[32,3,128]{2,1,0:T(4,128)S(1)} %copy.10.vel, s32[32]{0:T(128)S(1)} %copy-done.1, s32[32,4]{1,0:T(8,128)S(1)} %copy.11.near_ids, s32[5,4]{1,0:T(8,128)S(1)} %copy.12.export_ids, ...), custom_call_target="tpu_custom_call" | custom-call | tf_op jit(solution)/shard_map/pallas_call | solution.py:272
  61.8 0.6 copy.14
  62.4 0.6 copy.15
  (1 shorter events, 0.0 us)
Async XLA Ops:
  0.6 0.8 %copy-start.3 = (s32[20,4]{0,1:T(4,128)S(1)}, s32[20,4]{0,1:T(4,128)}, u32[]{:S(2)}) copy-start(s32[20,4]{0,1:T(4,128)} %param.13) | copy-start | bytes 964
  1.4 0.7 %copy-start.4 = (s32[32,4]{0,1:T(4,128)S(1)}, s32[32,4]{0,1:T(4,128)}, u32[]{:S(2)}) copy-start(s32[32,4]{0,1:T(4,128)} %param.11) | copy-start | bytes 1540
  2.2 0.8 %copy-start.2 = (f32[32,3,128]{2,0,1:T(8,128)S(1)}, f32[32,3,128]{2,0,1:T(8,128)}, u32[]{:S(2)}) copy-start(f32[32,3,128]{2,0,1:T(8,128)} %param.9) | copy-start | bytes 147460
  3.0 0.7 %copy-start = (f32[32,128]{1,0:T(8,128)S(1)}, f32[32,128]{1,0:T(8,128)}, u32[]{:S(2)}) copy-start(f32[32,128]{1,0:T(8,128)} %mass.1) | copy-start | bytes 49156
  3.1 0.7 %copy-start.1 = (s32[32]{0:T(128)S(1)}, s32[32]{0:T(128)}, u32[]{:S(2)}) copy-start(s32[32]{0:T(128)} %dest.1) | copy-start | bytes 388

commit v2 on v1

--- a/solution.py
+++ b/solution.py
@@ -18,12 +18,12 @@
 F32, BF16 = jnp.float32, jnp.bfloat16
 MESH = pl.DeviceIdType.MESH
 
-ALPHA = math.log2(math.e) / 0.36
+ALPHA = 4.009245535636174
 SOFT = ALPHA * 0.05**2
-N0, N1, N2, N3 = 8.53126995, 11.49321071, 11.59229692, 5.3254959
-D0, D1, D2 = 8.01883474, 10.80288261, 5.33752372
-LEAD = 0.9399344975074229
-SCALE = 0.01 * ALPHA**1.5 * LEAD
+N0, N1, N2, N3 = 638.3696617050974, 622.7581356810975, 614.039653607777, 155.2143515804912
+D0, D1 = 3.7186906578024175, 3.627694577131586
+LEAD = 0.005825292410791371
+SCALE = 0.01 * ALPHA**1.5 * LEAD * 2.0**SOFT
 KEEP = 48
 LATE = 12
 
@@ -43,13 +43,12 @@
     return total
 
 
-def weight(raw):
-    v = jnp.maximum(raw, 1e-30)
+def weight(t):
+    v = jnp.maximum(t - SOFT, 1e-30)
     u = v * lax.rsqrt(v)
-    t = v + SOFT
     upper = (((u + N3) * u + N2) * u + N1) * u + N0
-    lower = ((u + D2) * u + D1) * u + D0
-    p = t * lower * jnp.exp2(v)
+    lower = (u + D1) * u + D0
+    p = t * (lower * jnp.exp2(t))
     return upper * lax.rsqrt(p * p * t)
 
 
@@ -57,7 +56,7 @@
     row = lax.broadcasted_iota(jnp.int32, (8, BLOCK), 0)
     x = jnp.where(row < 3, x - 0.5, 0.0)
     norm = ALPHA * jnp.sum(x * x, axis=0, keepdims=True)
-    own = jnp.where(row < 3, x, jnp.where(row == 3, norm, jnp.where(row == 4, 1.0, 0.0)))
+    own = jnp.where(row < 3, x, jnp.where(row == 3, norm + SOFT, jnp.where(row == 4, 1.0, 0.0)))
     t1, t2, t3 = split3(own)
     return jnp.concatenate([t1, t2, t1, t2, t3, t1], axis=0).astype(BF16)
 
@@ -71,24 +70,20 @@
     s1, s2, s3 = split3(own)
     moment = (SCALE * mass) * jnp.where(row < 3, x, jnp.where(row == 3, 1.0, 0.0))
     m1, m2, m3 = split3(moment)
-    return (
-        jnp.concatenate([s1, s1, s2, s2, s1, s3], axis=0),
-        jnp.concatenate([m1, m2, m3, jnp.zeros_like(m1)], axis=0).astype(BF16),
-    )
+    moments = jnp.concatenate([m1, m2, m3, jnp.zeros_like(m1)], axis=0).astype(BF16)
+    return jnp.concatenate([s1, s1, s2, s2, s1, s3], axis=0), jnp.concatenate([moments, moments], axis=1)
 
 
 def pair_sum(x, features, source_ids, src, mom):
-    highs, lows, moments = [], [], []
-    for s in source_ids:
-        raw = jnp.dot(src[s][:, :KEEP], features, preferred_element_type=F32)
-        w = weight(raw)
+    sources = jnp.concatenate([src[s] for s in source_ids], axis=0)[:, :KEEP]
+    softened = jnp.dot(sources, features, preferred_element_type=F32)
+    a = None
+    for k, s in enumerate(source_ids):
+        w = weight(softened[k * BLOCK : (k + 1) * BLOCK])
         high = w.astype(BF16)
-        highs.append(high)
-        lows.append((w - high.astype(F32)).astype(BF16))
-        moments.append(mom[s])
-    moments = jnp.concatenate(moments, axis=1)
-    a = jnp.dot(moments, jnp.concatenate(highs, axis=0), preferred_element_type=F32)
-    a = a + jnp.dot(moments, jnp.concatenate(lows, axis=0), preferred_element_type=F32)
+        low = (w - high.astype(F32)).astype(BF16)
+        part = jnp.dot(mom[s], jnp.concatenate([high, low], axis=0), preferred_element_type=F32)
+        a = part if a is None else a + part
     a = a[0:8] + a[8:16] + a[16:24]
     return a - (x - 0.5) * a[3:4]
 
@@ -99,9 +94,9 @@
 
 
 def kernel(
-    domains, bits, pos, mass, vel, dest, near_ids, export_ids, far_ids, pos_out, vel_out,
-    pack_p, land_p, pack_v, land_v, new, tgt, src, mom, acc, out_x, in_x, out_a, in_a,
-    move_send, move_recv, x_send, x_recv, a_send, a_recv,
+    domains, bits, pos_in, mass_in, vel_in, dest, near_ids, export_ids, far_ids, pos_out, vel_out, acc_out,
+    pos, mass, vel, pack_p, land_p, pack_v, land_v, held_v, new, tgt, src, mom, acc, out_x, in_x, out_a, in_a,
+    move_send, move_recv, x_send, x_recv, a_send, a_recv, load,
 ):
     grp, dom = lax.axis_index("grp"), lax.axis_index("dom")
     inner = domains.bit_length() - 1
@@ -115,12 +110,19 @@
     barrier = pltpu.get_barrier_semaphore()
     outer = [bit for bit in bits if bit >= inner]
 
-    @pl.loop(1, domains)
+    @pl.loop(1, domains, unroll=9)
     def _(step):
         pl.semaphore_signal(barrier, inc=1, device_id=peer(step), device_id_type=MESH)
 
     for bit in outer:
         pl.semaphore_signal(barrier, inc=1, device_id=partner(bit), device_id_type=MESH)
+
+    loads = [
+        pltpu.make_async_copy(given, held, load.at[i])
+        for i, (given, held) in enumerate(((pos_in, pos), (mass_in, mass), (vel_in, vel)))
+    ]
+    for copy in loads:
+        copy.start()
 
     lane = lax.broadcasted_iota(jnp.int32, (1, BLOCK), 1)
     owner = lax.rem(lane, SLOTS)
@@ -161,14 +163,13 @@
         choice = jnp.where(count == key, 1.0, 0.0).astype(BF16)
         return exact_dot(choice, land.reshape(domains * 8, BLOCK)).reshape(SLOTS, 8, BLOCK)
 
-    pack_p[...] = packed(jnp.concatenate([pos[:, 0], pos[:, 1], pos[:, 2], mass[...]], axis=0))
-    pack_v[...] = packed(
-        jnp.concatenate([vel[:, 0], vel[:, 1], vel[:, 2], jnp.zeros((SLOTS, BLOCK), F32)], axis=0)
-    )
+    for copy in loads:
+        copy.wait()
+    pack_p[...] = packed(jnp.concatenate([pos[0], pos[1], pos[2], mass[...]], axis=0))
     pl.semaphore_wait(barrier, domains - 1 + len(outer))
 
     def move(pack, land, k):
-        @pl.loop(1, domains)
+        @pl.loop(1, domains, unroll=9)
         def _(step):
             pltpu.make_async_remote_copy(
                 src_ref=pack.at[step], dst_ref=land.at[step],
@@ -184,7 +185,9 @@
         )
 
     move(pack_p, land_p, 0)
-    move(pack_v, land_v, 1)
+    pack_v[...] = packed(
+        jnp.concatenate([vel[0], vel[1], vel[2], jnp.zeros((SLOTS, BLOCK), F32)], axis=0)
+    )
     land_p[0] = pack_p[0]
     land_v[0] = pack_v[0]
     moved(pack_p, land_p, 0).wait_recv()
@@ -204,8 +207,10 @@
 
     for r in range(ROUNDS):
         for e in range(EXPORTS):
-            out_x[r, e] = new[export_ids[r, e]]
+            out_x[r, e] = new[export_ids[e, r]]
         visit(r).start()
+
+    move(pack_v, land_v, 1)
 
     def prepare(b, carry):
         x = new[b]
@@ -218,22 +223,22 @@
     lax.fori_loop(0, SLOTS, prepare, 0, unroll=4)
 
     def near(b, carry):
-        acc[b] = pair_sum(new[b], tgt[b], [near_ids[b, k] for k in range(NEAR)], src, mom)
+        acc[b] = pair_sum(new[b], tgt[b], [near_ids[k, b] for k in range(NEAR)], src, mom)
         return carry
 
-    lax.fori_loop(0, SLOTS - LATE, near, 0, unroll=4)
+    lax.fori_loop(0, SLOTS - LATE, near, 0, unroll=10)
     for r in range(ROUNDS):
         visit(r).wait_recv()
 
         def far(e, carry, r=r):
             x = in_x[r, e]
-            ids = [far_ids[r * EXPORTS + e, k] for k in range(FAR)]
+            ids = [far_ids[k, r * EXPORTS + e] for k in range(FAR)]
             out_a[r, e] = pair_sum(x, target_rows(x), ids, src, mom)
             return carry
 
         lax.fori_loop(0, EXPORTS, far, 0, unroll=4)
         give_back(r).start()
-    lax.fori_loop(SLOTS - LATE, SLOTS, near, 0, unroll=4)
+    lax.fori_loop(SLOTS - LATE, SLOTS, near, 0, unroll=6)
 
     moved(pack_v, land_v, 1).wait_recv()
     new_vel = unpacked(land_v[...])
@@ -242,7 +247,7 @@
     for r in range(ROUNDS):
         give_back(r).wait_recv()
         for e in range(EXPORTS):
-            slot = jnp.where(lax.div(wide, 8) == r * EXPORTS + e, export_ids[r, e], slot)
+            slot = jnp.where(lax.div(wide, 8) == r * EXPORTS + e, export_ids[e, r], slot)
     rows8 = lax.broadcasted_iota(jnp.int32, (SLOTS * 8, 256), 0)
     wide8 = lax.broadcasted_iota(jnp.int32, (SLOTS * 8, 256), 1)
     hit = (lax.div(rows8, 8) == slot) & (lax.rem(rows8, 8) == lax.rem(wide8, 8))
@@ -250,10 +255,12 @@
         [in_a[...].reshape(ROUNDS * EXPORTS * 8, BLOCK), jnp.zeros((256 - ROUNDS * EXPORTS * 8, BLOCK), F32)], axis=0
     )
     far_acc = exact_dot(jnp.where(hit, 1.0, 0.0).astype(BF16), returned).reshape(SLOTS, 8, BLOCK)
-    new_vel = new_vel + TIMESTEP * (acc[...] + far_acc)
-    new_pos = new[...] + TIMESTEP * new_vel
-    pos_out[...] = new_pos[:, :3]
-    vel_out[...] = new_vel[:, :3]
+    acc[...] = acc[...] + far_acc
+    held_v[...] = new_vel
+    for c in range(3):
+        pos_out[c] = new[:, c]
+        vel_out[c] = held_v[:, c]
+        acc_out[c] = acc[:, c]
     for r in range(ROUNDS):
         visit(r).wait_send()
         give_back(r).wait_send()
@@ -266,33 +273,40 @@
     devices = domains * lax.axis_size("grp")
     levels = devices.bit_length() - 1
     bits = [r * levels // ROUNDS for r in range(ROUNDS)]
-    vmem, smem = pl.BlockSpec(memory_space=pltpu.VMEM), pl.BlockSpec(memory_space=pltpu.SMEM)
+    hbm, vmem = pl.BlockSpec(memory_space=pltpu.HBM), pl.BlockSpec(memory_space=pltpu.VMEM)
+    smem = pl.BlockSpec(memory_space=pltpu.SMEM)
     moves = pltpu.VMEM((domains, 8, BLOCK), F32)
     visits = pltpu.VMEM((ROUNDS, EXPORTS, 8, BLOCK), F32)
-    return pl.pallas_call(
+    across = (1, 0, 2)
+    outs = pl.pallas_call(
         functools.partial(kernel, domains, bits),
-        out_shape=(
-            jax.ShapeDtypeStruct(positions.shape, F32),
-            jax.ShapeDtypeStruct(velocities.shape, F32),
-        ),
-        in_specs=[vmem] * 3 + [smem] * 4,
-        out_specs=(vmem, vmem),
+        out_shape=(jax.ShapeDtypeStruct((3, SLOTS, BLOCK), F32),) * 3,
+        in_specs=[hbm] * 3 + [smem] * 4,
+        out_specs=(vmem,) * 3,
         scratch_shapes=[
+            pltpu.VMEM((3, SLOTS, BLOCK), F32), pltpu.VMEM((SLOTS, BLOCK), F32), pltpu.VMEM((3, SLOTS, BLOCK), F32),
             moves, moves, moves, moves,
+            pltpu.VMEM((SLOTS, 8, BLOCK), F32),
             pltpu.VMEM((SLOTS, 8, BLOCK), F32),
             pltpu.VMEM((SLOTS, KEEP, BLOCK), BF16),
             pltpu.VMEM((SLOTS, BLOCK, BLOCK), BF16),
-            pltpu.VMEM((SLOTS, 32, BLOCK), BF16),
+            pltpu.VMEM((SLOTS, 32, 2 * BLOCK), BF16),
             pltpu.VMEM((SLOTS, 8, BLOCK), F32),
             visits, visits, visits, visits,
             pltpu.SemaphoreType.DMA((2,)), pltpu.SemaphoreType.DMA((2,)),
             pltpu.SemaphoreType.DMA((ROUNDS,)), pltpu.SemaphoreType.DMA((ROUNDS,)),
-            pltpu.SemaphoreType.DMA((ROUNDS,)), pltpu.SemaphoreType.DMA((ROUNDS,)),
+            pltpu.SemaphoreType.DMA((ROUNDS,)), pltpu.SemaphoreType.DMA((ROUNDS,)), pltpu.SemaphoreType.DMA((3,)),
         ],
         compiler_params=pltpu.CompilerParams(
-            collective_id=0, has_side_effects=True, vmem_limit_bytes=40 * 2**20
+            collective_id=0, has_side_effects=True, vmem_limit_bytes=60 * 2**20
         ),
-    )(positions, masses, velocities, dest_dom, local_pairs, export_list, cross_pairs)
+    )(
+        positions.transpose(across), masses, velocities.transpose(across), dest_dom,
+        local_pairs.T, export_list.T, cross_pairs.T,
+    )
+    new_pos, new_vel, acceleration = (out.transpose(across) for out in outs)
+    vel_out = new_vel + TIMESTEP * acceleration
+    return new_pos + TIMESTEP * vel_out, vel_out
 
 
 def solution(mesh):

time: 63.3 us -> 54.7 us (0.86)
  the two profiles are of different devices: /device:TPU:8 before, /device:TPU:14 now
where the time goes in v2:
time: 54.7 us; the launch traced here: 54.4 us
  Pallas kernels  52.3 us (96%)
  other arithmetic  1.49 us (3%)
  between operations  0.64 us (1%)
    pallas_call x1, Pallas kernels, on_device(): pl.pallas_call(functools.partial(kernel, domains, bits), out_shape=(jax.S...  52.3 us
    add x1, other arithmetic, on_device(): return (new_pos + TIMESTEP * vel_out, vel_out)  1.49 us

profile of v2, /device:TPU:14, one launch (start us, length us, event | category | flops | bytes accessed | tf_op | source)
XLA Modules:
  0.0 54.4 jit_solution(13240784544600190337)
XLA Ops:
  0.6 52.3 %shard_map.86 = (f32[3,32,128]{2,1,0:T(8,128)}, f32[3,32,128]{2,1,0:T(8,128)}, f32[3,32,128]{2,1,0:T(8,128)}) custom-call(f32[3,32,128]{2,1,0:T(8,128)} %bitcast.10, f32[32,128]{1,0:T(8,128)} %mass_in.1, f32[3,32,128]{2,1,0:T(8,128)} %bitcast.11, s32[32]{0:T(128)} %dest.1, s32[4,32]{1,0:T(4,128)} %bitcast.12, s32[4,5]{1,0:T(4,128)} %bitcast.13, s32[4,20]{1,0:T(4,128)} %bitcast.14), custom_call_target="tpu_custom_call" | custom-call | tf_op jit(solution)/shard_map/pallas_call | solution.py:281
  52.9 1.5 %bitcast_add_fusion = (f32[32,3,128]{2,0,1:T(8,128)}, f32[32,3,128]{2,0,1:T(8,128)}) fusion(f32[3,32,128]{2,1,0:T(8,128)} %get-tuple-element.5, f32[3,32,128]{2,1,0:T(8,128)} %get-tuple-element.6, f32[3,32,128]{2,1,0:T(8,128)} %get-tuple-element.7), kind=kLoop, calls=%fused_computation | loop fusion | flops 49152 | bytes 245760 | tf_op jit(solution)/shard_map/add | solution.py:309

commit v3 on v2

--- a/solution.py
+++ b/solution.py
@@ -25,6 +25,8 @@
 LEAD = 0.005825292410791371
 SCALE = 0.01 * ALPHA**1.5 * LEAD * 2.0**SOFT
 KEEP = 48
+FETCH = 2
+ORDER = (3, 1, 4, 0)
 LATE = 12
 
 
@@ -95,7 +97,7 @@
 
 def kernel(
     domains, bits, pos_in, mass_in, vel_in, dest, near_ids, export_ids, far_ids, pos_out, vel_out, acc_out,
-    pos, mass, vel, pack_p, land_p, pack_v, land_v, held_v, new, tgt, src, mom, acc, out_x, in_x, out_a, in_a,
+    pos, mass, vel, pack_p, land_p, pack_v, land_v, new, tgt, src, mom, acc, out_f, in_f, out_x, in_x, out_a, in_a,
     move_send, move_recv, x_send, x_recv, a_send, a_recv, load,
 ):
     grp, dom = lax.axis_index("grp"), lax.axis_index("dom")
@@ -104,14 +106,25 @@
     def partner(bit):
         return (grp, flipped(dom, bit)) if bit < inner else (flipped(grp, bit - inner), dom)
 
+    columns = domains // 4
+
     def peer(step):
         return (grp, lax.rem(dom + step, domains))
 
+    def far_first(j):
+        a = lax.div(j, 4)
+        along = columns // 2 + (1 - 2 * lax.rem(a, 2)) * lax.div(a + 1, 2)
+        return lax.rem(j, 4) * columns + along
+
     barrier = pltpu.get_barrier_semaphore()
     outer = [bit for bit in bits if bit >= inner]
-
-    @pl.loop(1, domains, unroll=9)
-    def _(step):
+    land_v[:, pl.ds(6, 2)] = jnp.zeros((domains, 2, BLOCK), F32)
+
+    def greet(j):
+        pl.semaphore_signal(barrier, inc=1, device_id=peer(far_first(j)), device_id_type=MESH)
+
+    pl.loop(0, domains - 4, unroll=10)(greet)
+    for step in range(columns, domains, columns):
         pl.semaphore_signal(barrier, inc=1, device_id=peer(step), device_id_type=MESH)
 
     for bit in outer:
@@ -141,57 +154,59 @@
     rank = jnp.sum(jnp.where(same, 1.0, 0.0), axis=0, keepdims=True)
     away = lax.rem(target - dom + domains, domains)
     away_f = away.astype(F32)
-    base = away_f * 8.0 + rank * 4.0
     came_from = lax.rem(dom - away + domains, domains).astype(F32) * 2.0 + rank
     place = jnp.sum(jnp.where(as_column(came_from) < came_from, 1.0, 0.0), axis=0, keepdims=True)
 
-    def packed(stacked):
-        key = base + lax.div(lane, SLOTS).astype(F32)
+    def packed(stacked, stride):
+        key = away_f * 8.0 + rank * stride + lax.div(lane, SLOTS).astype(F32)
         count = lax.broadcasted_iota(jnp.int32, (domains * 8, BLOCK), 0).astype(F32)
         choice = jnp.where(count == key, 1.0, 0.0).astype(BF16)
         return exact_dot(choice, stacked).reshape(domains, 8, BLOCK)
 
-    row8 = lax.broadcasted_iota(jnp.int32, (SLOTS * 8, BLOCK), 0)
-    lane8 = lax.broadcasted_iota(jnp.int32, (SLOTS * 8, BLOCK), 1)
-    found = (lane8 < SLOTS) & (place == lax.div(row8, 8).astype(F32))
-    key = jnp.sum(jnp.where(found, base, 0.0), axis=1, keepdims=True)
-    part = lax.rem(lax.broadcasted_iota(jnp.int32, (SLOTS * 8, 1), 0), 8)
-    key = jnp.where(part < 4, key + part.astype(F32), -1.0)
-
-    def unpacked(land):
-        count = lax.broadcasted_iota(jnp.int32, (SLOTS * 8, domains * 8), 1).astype(F32)
+    def unpacked(land, slot, part, stride):
+        rows = slot.shape[0]
+        first = lax.broadcasted_iota(jnp.int32, (rows, BLOCK), 1) < SLOTS
+        key = jnp.sum(jnp.where(first & (place == slot), away_f * 8.0 + rank * stride, 0.0), axis=1, keepdims=True)
+        key = jnp.where(part < stride, key + part, -1.0)
+        count = lax.broadcasted_iota(jnp.int32, (rows, domains * 8), 1).astype(F32)
         choice = jnp.where(count == key, 1.0, 0.0).astype(BF16)
-        return exact_dot(choice, land.reshape(domains * 8, BLOCK)).reshape(SLOTS, 8, BLOCK)
+        return exact_dot(choice, land.reshape(domains * 8, BLOCK))
 
     for copy in loads:
         copy.wait()
-    pack_p[...] = packed(jnp.concatenate([pos[0], pos[1], pos[2], mass[...]], axis=0))
+    pack_p[...] = packed(jnp.concatenate([pos[0], pos[1], pos[2], mass[...]], axis=0), 4.0)
     pl.semaphore_wait(barrier, domains - 1 + len(outer))
 
-    def move(pack, land, k):
-        @pl.loop(1, domains, unroll=9)
-        def _(step):
+    def move(pack, land, k, rows):
+        def send(step):
             pltpu.make_async_remote_copy(
-                src_ref=pack.at[step], dst_ref=land.at[step],
+                src_ref=pack.at[step, pl.ds(0, rows)], dst_ref=land.at[step, pl.ds(0, rows)],
                 send_sem=move_send.at[k], recv_sem=move_recv.at[k],
                 device_id=peer(step), device_id_type=MESH,
             ).start()
 
-    def moved(pack, land, k):
+        pl.loop(0, domains - 4, unroll=10)(lambda j: send(far_first(j)))
+        for step in range(columns, domains, columns):
+            send(step)
+
+    def moved(pack, land, k, rows):
         return pltpu.make_async_remote_copy(
-            src_ref=pack.at[pl.ds(1, domains - 1)], dst_ref=land.at[pl.ds(1, domains - 1)],
+            src_ref=pack.at[pl.ds(1, domains - 1), pl.ds(0, rows)],
+            dst_ref=land.at[pl.ds(1, domains - 1), pl.ds(0, rows)],
             send_sem=move_send.at[k], recv_sem=move_recv.at[k],
             device_id=peer(1), device_id_type=MESH,
         )
 
-    move(pack_p, land_p, 0)
+    move(pack_p, land_p, 0, 8)
     pack_v[...] = packed(
-        jnp.concatenate([vel[0], vel[1], vel[2], jnp.zeros((SLOTS, BLOCK), F32)], axis=0)
+        jnp.concatenate([vel[0], vel[1], vel[2], jnp.zeros((SLOTS, BLOCK), F32)], axis=0), 3.0
     )
     land_p[0] = pack_p[0]
     land_v[0] = pack_v[0]
-    moved(pack_p, land_p, 0).wait_recv()
-    new[...] = unpacked(land_p[...])
+    moved(pack_p, land_p, 0, 8).wait_recv()
+    row8 = lax.broadcasted_iota(jnp.int32, (SLOTS * 8, 1), 0)
+    slot8, part8 = lax.div(row8, 8).astype(F32), lax.rem(row8, 8).astype(F32)
+    new[...] = unpacked(land_p[...], slot8, part8, 4.0).reshape(SLOTS, 8, BLOCK)
 
     def visit(r):
         return pltpu.make_async_remote_copy(
@@ -205,19 +220,29 @@
             device_id=partner(bits[r]), device_id_type=MESH,
         )
 
-    for r in range(ROUNDS):
+    fetch = pltpu.make_async_remote_copy(
+        src_ref=out_f, dst_ref=in_f, send_sem=x_send.at[FETCH], recv_sem=x_recv.at[FETCH],
+        device_id=partner(bits[FETCH]), device_id_type=MESH,
+    )
+    for i in range(EXPORTS * FAR):
+        out_f[i // 2, pl.ds(i % 2 * 4, 4)] = new[far_ids[i % FAR, FETCH * EXPORTS + i // FAR], pl.ds(0, 4)]
+    fetch.start()
+    for r in ORDER:
         for e in range(EXPORTS):
-            out_x[r, e] = new[export_ids[e, r]]
+            out_x[r, e // 2, pl.ds(e % 2 * 4, 4)] = new[export_ids[e, r], pl.ds(0, 4)]
         visit(r).start()
 
-    move(pack_v, land_v, 1)
+    move(pack_v, land_v, 1, 6)
+
+    def as_source(x, b):
+        features, moments = source_rows(x)
+        src[b] = jnp.concatenate([features, jnp.zeros((BLOCK - KEEP, BLOCK), F32)], axis=0).T.astype(BF16)
+        mom[b] = moments
 
     def prepare(b, carry):
         x = new[b]
         tgt[b] = target_rows(x)
-        features, moments = source_rows(x)
-        src[b] = jnp.concatenate([features, jnp.zeros((BLOCK - KEEP, BLOCK), F32)], axis=0).T.astype(BF16)
-        mom[b] = moments
+        as_source(x, b)
         return carry
 
     lax.fori_loop(0, SLOTS, prepare, 0, unroll=4)
@@ -227,45 +252,47 @@
         return carry
 
     lax.fori_loop(0, SLOTS - LATE, near, 0, unroll=10)
-    for r in range(ROUNDS):
+    for r in ORDER:
         visit(r).wait_recv()
-
-        def far(e, carry, r=r):
-            x = in_x[r, e]
+        for e in range(EXPORTS):
+            x = in_x[r, e // 2, pl.ds(e % 2 * 4, 4)]
+            x = jnp.concatenate([x, jnp.zeros_like(x)], axis=0)
             ids = [far_ids[k, r * EXPORTS + e] for k in range(FAR)]
-            out_a[r, e] = pair_sum(x, target_rows(x), ids, src, mom)
-            return carry
-
-        lax.fori_loop(0, EXPORTS, far, 0, unroll=4)
+            out_a[r, e // 2, pl.ds(e % 2 * 4, 4)] = pair_sum(x, target_rows(x), ids, src, mom)[0:4]
         give_back(r).start()
     lax.fori_loop(SLOTS - LATE, SLOTS, near, 0, unroll=6)
-
-    moved(pack_v, land_v, 1).wait_recv()
-    new_vel = unpacked(land_v[...])
-    wide = lax.broadcasted_iota(jnp.int32, (1, 256), 1)
-    slot = jnp.full((1, 256), -1, jnp.int32)
+    fetch.wait_recv()
+    for i in range(EXPORTS * FAR):
+        x = in_f[i // 2, pl.ds(i % 2 * 4, 4)]
+        as_source(jnp.concatenate([x, jnp.zeros_like(x)], axis=0), SLOTS + i)
+    for e in range(EXPORTS):
+        b = export_ids[e, FETCH]
+        ids = [SLOTS + e * FAR + k for k in range(FAR)]
+        in_a[FETCH, e // 2, pl.ds(e % 2 * 4, 4)] = pair_sum(new[b], tgt[b], ids, src, mom)[0:4]
+
+    moved(pack_v, land_v, 1, 6).wait_recv()
+    row3 = lax.broadcasted_iota(jnp.int32, (SLOTS * 3, 1), 0)
+    slot3, part3 = lax.rem(row3, SLOTS), lax.div(row3, SLOTS)
+    vel_out[...] = unpacked(land_v[...], slot3.astype(F32), part3.astype(F32), 3.0).reshape(3, SLOTS, BLOCK)
+    exported = jnp.full((1, BLOCK), -1, jnp.int32)
     for r in range(ROUNDS):
-        give_back(r).wait_recv()
+        if r != FETCH:
+            give_back(r).wait_recv()
         for e in range(EXPORTS):
-            slot = jnp.where(lax.div(wide, 8) == r * EXPORTS + e, export_ids[e, r], slot)
-    rows8 = lax.broadcasted_iota(jnp.int32, (SLOTS * 8, 256), 0)
-    wide8 = lax.broadcasted_iota(jnp.int32, (SLOTS * 8, 256), 1)
-    hit = (lax.div(rows8, 8) == slot) & (lax.rem(rows8, 8) == lax.rem(wide8, 8))
-    returned = jnp.concatenate(
-        [in_a[...].reshape(ROUNDS * EXPORTS * 8, BLOCK), jnp.zeros((256 - ROUNDS * EXPORTS * 8, BLOCK), F32)], axis=0
-    )
-    far_acc = exact_dot(jnp.where(hit, 1.0, 0.0).astype(BF16), returned).reshape(SLOTS, 8, BLOCK)
-    acc[...] = acc[...] + far_acc
-    held_v[...] = new_vel
+            exported = jnp.where(lax.div(lane, 4) == r * EXPORTS + e, export_ids[e, r], exported)
+    hit = (slot3 == exported) & (part3 == lax.rem(lane, 4))
+    returned = in_a[...].reshape(ROUNDS * EXPORTS * 4, BLOCK)
+    returned = jnp.concatenate([returned, jnp.zeros((BLOCK - ROUNDS * EXPORTS * 4, BLOCK), F32)], axis=0)
+    far_acc = exact_dot(jnp.where(hit, 1.0, 0.0).astype(BF16), returned).reshape(3, SLOTS, BLOCK)
     for c in range(3):
         pos_out[c] = new[:, c]
-        vel_out[c] = held_v[:, c]
-        acc_out[c] = acc[:, c]
-    for r in range(ROUNDS):
+        acc_out[c] = acc[:, c] + far_acc[c]
+    fetch.wait_send()
+    for r in ORDER:
         visit(r).wait_send()
         give_back(r).wait_send()
-    moved(pack_p, land_p, 0).wait_send()
-    moved(pack_v, land_v, 1).wait_send()
+    moved(pack_p, land_p, 0, 8).wait_send()
+    moved(pack_v, land_v, 1, 6).wait_send()
 
 
 def on_device(positions, masses, velocities, dest_dom, local_pairs, export_list, cross_pairs):
@@ -276,7 +303,7 @@
     hbm, vmem = pl.BlockSpec(memory_space=pltpu.HBM), pl.BlockSpec(memory_space=pltpu.VMEM)
     smem = pl.BlockSpec(memory_space=pltpu.SMEM)
     moves = pltpu.VMEM((domains, 8, BLOCK), F32)
-    visits = pltpu.VMEM((ROUNDS, EXPORTS, 8, BLOCK), F32)
+    visits = pltpu.VMEM((ROUNDS, EXPORTS // 2, 8, BLOCK), F32)
     across = (1, 0, 2)
     outs = pl.pallas_call(
         functools.partial(kernel, domains, bits),
@@ -287,11 +314,11 @@
             pltpu.VMEM((3, SLOTS, BLOCK), F32), pltpu.VMEM((SLOTS, BLOCK), F32), pltpu.VMEM((3, SLOTS, BLOCK), F32),
             moves, moves, moves, moves,
             pltpu.VMEM((SLOTS, 8, BLOCK), F32),
+            pltpu.VMEM((SLOTS, KEEP, BLOCK), BF16),
+            pltpu.VMEM((SLOTS + EXPORTS * FAR, BLOCK, BLOCK), BF16),
+            pltpu.VMEM((SLOTS + EXPORTS * FAR, 32, 2 * BLOCK), BF16),
             pltpu.VMEM((SLOTS, 8, BLOCK), F32),
-            pltpu.VMEM((SLOTS, KEEP, BLOCK), BF16),
-            pltpu.VMEM((SLOTS, BLOCK, BLOCK), BF16),
-            pltpu.VMEM((SLOTS, 32, 2 * BLOCK), BF16),
-            pltpu.VMEM((SLOTS, 8, BLOCK), F32),
+            pltpu.VMEM((EXPORTS * FAR // 2, 8, BLOCK), F32), pltpu.VMEM((EXPORTS * FAR // 2, 8, BLOCK), F32),
             visits, visits, visits, visits,
             pltpu.SemaphoreType.DMA((2,)), pltpu.SemaphoreType.DMA((2,)),
             pltpu.SemaphoreType.DMA((ROUNDS,)), pltpu.SemaphoreType.DMA((ROUNDS,)),

time: 54.7 us -> 51 us (0.932)
  the two profiles are of different devices: /device:TPU:14 before, /device:TPU:1 now
where the time goes in v3:
time: 51 us; the launch traced here: 50.7 us
  Pallas kernels  48.6 us (95%)
  other arithmetic  1.49 us (3%)
  between operations  0.64 us (1%)
    pallas_call x1, Pallas kernels, on_device(): pl.pallas_call(functools.partial(kernel, domains, bits), out_shape=(jax.S...  48.6 us
    add x1, other arithmetic, on_device(): return (new_pos + TIMESTEP * vel_out, vel_out)  1.49 us

profile of v3, /device:TPU:1, one launch (start us, length us, event | category | flops | bytes accessed | tf_op | source)
XLA Modules:
  0.0 50.7 jit_solution(9636631085968361052)
XLA Ops:
  0.6 48.6 %shard_map.86 = (f32[3,32,128]{2,1,0:T(8,128)}, f32[3,32,128]{2,1,0:T(8,128)}, f32[3,32,128]{2,1,0:T(8,128)}) custom-call(f32[3,32,128]{2,1,0:T(8,128)} %bitcast.10, f32[32,128]{1,0:T(8,128)} %mass_in.1, f32[3,32,128]{2,1,0:T(8,128)} %bitcast.11, s32[32]{0:T(128)} %dest.1, s32[4,32]{1,0:T(4,128)} %bitcast.12, s32[4,5]{1,0:T(4,128)} %bitcast.13, s32[4,20]{1,0:T(4,128)} %bitcast.14), custom_call_target="tpu_custom_call" | custom-call | tf_op jit(solution)/shard_map/pallas_call | solution.py:308
  49.2 1.5 %bitcast_add_fusion = (f32[32,3,128]{2,0,1:T(8,128)}, f32[32,3,128]{2,0,1:T(8,128)}) fusion(f32[3,32,128]{2,1,0:T(8,128)} %get-tuple-element.5, f32[3,32,128]{2,1,0:T(8,128)} %get-tuple-element.6, f32[3,32,128]{2,1,0:T(8,128)} %get-tuple-element.7), kind=kLoop, calls=%fused_computation | loop fusion | flops 49152 | bytes 245760 | tf_op jit(solution)/shard_map/add | solution.py:336

commit v4 on v3

--- a/solution.py
+++ b/solution.py
@@ -97,7 +97,7 @@
 
 def kernel(
     domains, bits, pos_in, mass_in, vel_in, dest, near_ids, export_ids, far_ids, pos_out, vel_out, acc_out,
-    pos, mass, vel, pack_p, land_p, pack_v, land_v, new, tgt, src, mom, acc, out_f, in_f, out_x, in_x, out_a, in_a,
+    pos, mass, vel, pack_p, land_p, pack_v, land_v, pick_p, pick_v, pick_a, new, tgt, src, mom, acc, out_f, in_f, out_x, in_x, out_a, in_a,
     move_send, move_recv, x_send, x_recv, a_send, a_recv, load,
 ):
     grp, dom = lax.axis_index("grp"), lax.axis_index("dom")
@@ -109,24 +109,17 @@
     columns = domains // 4
 
     def peer(step):
-        return (grp, lax.rem(dom + step, domains))
-
-    def far_first(j):
-        a = lax.div(j, 4)
-        along = columns // 2 + (1 - 2 * lax.rem(a, 2)) * lax.div(a + 1, 2)
-        return lax.rem(j, 4) * columns + along
+        there = dom + step
+        return (grp, jnp.where(there >= domains, there - domains, there))
+
+    steps = sorted(range(1, domains), key=lambda d: -min(d % columns, -d % columns))
 
     barrier = pltpu.get_barrier_semaphore()
     outer = [bit for bit in bits if bit >= inner]
     land_v[:, pl.ds(6, 2)] = jnp.zeros((domains, 2, BLOCK), F32)
 
-    def greet(j):
-        pl.semaphore_signal(barrier, inc=1, device_id=peer(far_first(j)), device_id_type=MESH)
-
-    pl.loop(0, domains - 4, unroll=10)(greet)
-    for step in range(columns, domains, columns):
+    for step in steps:
         pl.semaphore_signal(barrier, inc=1, device_id=peer(step), device_id_type=MESH)
-
     for bit in outer:
         pl.semaphore_signal(barrier, inc=1, device_id=partner(bit), device_id_type=MESH)
 
@@ -163,14 +156,13 @@
         choice = jnp.where(count == key, 1.0, 0.0).astype(BF16)
         return exact_dot(choice, stacked).reshape(domains, 8, BLOCK)
 
-    def unpacked(land, slot, part, stride):
+    def arrivals(slot, part, stride):
         rows = slot.shape[0]
         first = lax.broadcasted_iota(jnp.int32, (rows, BLOCK), 1) < SLOTS
         key = jnp.sum(jnp.where(first & (place == slot), away_f * 8.0 + rank * stride, 0.0), axis=1, keepdims=True)
         key = jnp.where(part < stride, key + part, -1.0)
         count = lax.broadcasted_iota(jnp.int32, (rows, domains * 8), 1).astype(F32)
-        choice = jnp.where(count == key, 1.0, 0.0).astype(BF16)
-        return exact_dot(choice, land.reshape(domains * 8, BLOCK))
+        return jnp.where(count == key, 1.0, 0.0).astype(BF16)
 
     for copy in loads:
         copy.wait()
@@ -178,16 +170,12 @@
     pl.semaphore_wait(barrier, domains - 1 + len(outer))
 
     def move(pack, land, k, rows):
-        def send(step):
+        for step in steps:
             pltpu.make_async_remote_copy(
                 src_ref=pack.at[step, pl.ds(0, rows)], dst_ref=land.at[step, pl.ds(0, rows)],
                 send_sem=move_send.at[k], recv_sem=move_recv.at[k],
                 device_id=peer(step), device_id_type=MESH,
             ).start()
-
-        pl.loop(0, domains - 4, unroll=10)(lambda j: send(far_first(j)))
-        for step in range(columns, domains, columns):
-            send(step)
 
     def moved(pack, land, k, rows):
         return pltpu.make_async_remote_copy(
@@ -203,10 +191,19 @@
     )
     land_p[0] = pack_p[0]
     land_v[0] = pack_v[0]
+    row8 = lax.broadcasted_iota(jnp.int32, (SLOTS * 8, 1), 0)
+    pick_p[...] = arrivals(lax.div(row8, 8).astype(F32), lax.rem(row8, 8).astype(F32), 4.0)
+    row3 = lax.broadcasted_iota(jnp.int32, (SLOTS * 3, 1), 0)
+    slot3, part3 = lax.rem(row3, SLOTS), lax.div(row3, SLOTS)
+    pick_v[...] = arrivals(slot3.astype(F32), part3.astype(F32), 3.0)
+    exported = jnp.full((1, BLOCK), -1, jnp.int32)
+    for r in range(ROUNDS):
+        for e in range(EXPORTS):
+            exported = jnp.where(lax.div(lane, 4) == r * EXPORTS + e, export_ids[e, r], exported)
+    hit = (slot3 == exported) & (part3 == lax.rem(lane, 4))
+    pick_a[...] = jnp.where(hit, 1.0, 0.0).astype(BF16)
     moved(pack_p, land_p, 0, 8).wait_recv()
-    row8 = lax.broadcasted_iota(jnp.int32, (SLOTS * 8, 1), 0)
-    slot8, part8 = lax.div(row8, 8).astype(F32), lax.rem(row8, 8).astype(F32)
-    new[...] = unpacked(land_p[...], slot8, part8, 4.0).reshape(SLOTS, 8, BLOCK)
+    new[...] = exact_dot(pick_p[...], land_p[...].reshape(domains * 8, BLOCK)).reshape(SLOTS, 8, BLOCK)
 
     def visit(r):
         return pltpu.make_async_remote_copy(
@@ -252,14 +249,27 @@
         return carry
 
     lax.fori_loop(0, SLOTS - LATE, near, 0, unroll=10)
-    for r in ORDER:
-        visit(r).wait_recv()
+    @pl.loop(0, len(ORDER))
+    def _(j):
+        r = ORDER[0]
+        for n, m in enumerate(ORDER):
+            r = jnp.where(j == n, m, r)
+
+            @pl.when(j == n)
+            def _(m=m):
+                visit(m).wait_recv()
+
         for e in range(EXPORTS):
             x = in_x[r, e // 2, pl.ds(e % 2 * 4, 4)]
             x = jnp.concatenate([x, jnp.zeros_like(x)], axis=0)
             ids = [far_ids[k, r * EXPORTS + e] for k in range(FAR)]
             out_a[r, e // 2, pl.ds(e % 2 * 4, 4)] = pair_sum(x, target_rows(x), ids, src, mom)[0:4]
-        give_back(r).start()
+        for n, m in enumerate(ORDER):
+
+            @pl.when(j == n)
+            def _(m=m):
+                give_back(m).start()
+
     lax.fori_loop(SLOTS - LATE, SLOTS, near, 0, unroll=6)
     fetch.wait_recv()
     for i in range(EXPORTS * FAR):
@@ -270,23 +280,17 @@
         ids = [SLOTS + e * FAR + k for k in range(FAR)]
         in_a[FETCH, e // 2, pl.ds(e % 2 * 4, 4)] = pair_sum(new[b], tgt[b], ids, src, mom)[0:4]
 
-    moved(pack_v, land_v, 1, 6).wait_recv()
-    row3 = lax.broadcasted_iota(jnp.int32, (SLOTS * 3, 1), 0)
-    slot3, part3 = lax.rem(row3, SLOTS), lax.div(row3, SLOTS)
-    vel_out[...] = unpacked(land_v[...], slot3.astype(F32), part3.astype(F32), 3.0).reshape(3, SLOTS, BLOCK)
-    exported = jnp.full((1, BLOCK), -1, jnp.int32)
-    for r in range(ROUNDS):
-        if r != FETCH:
-            give_back(r).wait_recv()
-        for e in range(EXPORTS):
-            exported = jnp.where(lax.div(lane, 4) == r * EXPORTS + e, export_ids[e, r], exported)
-    hit = (slot3 == exported) & (part3 == lax.rem(lane, 4))
+    for r in ORDER:
+        give_back(r).wait_recv()
     returned = in_a[...].reshape(ROUNDS * EXPORTS * 4, BLOCK)
     returned = jnp.concatenate([returned, jnp.zeros((BLOCK - ROUNDS * EXPORTS * 4, BLOCK), F32)], axis=0)
-    far_acc = exact_dot(jnp.where(hit, 1.0, 0.0).astype(BF16), returned).reshape(3, SLOTS, BLOCK)
+    far_acc = exact_dot(pick_a[...], returned).reshape(3, SLOTS, BLOCK)
     for c in range(3):
         pos_out[c] = new[:, c]
         acc_out[c] = acc[:, c] + far_acc[c]
+    moved(pack_v, land_v, 1, 6).wait_recv()
+    new_vel = exact_dot(pick_v[...], land_v[...].reshape(domains * 8, BLOCK))
+    vel_out[...] = new_vel.reshape(3, SLOTS, BLOCK)
     fetch.wait_send()
     for r in ORDER:
         visit(r).wait_send()
@@ -313,6 +317,8 @@
         scratch_shapes=[
             pltpu.VMEM((3, SLOTS, BLOCK), F32), pltpu.VMEM((SLOTS, BLOCK), F32), pltpu.VMEM((3, SLOTS, BLOCK), F32),
             moves, moves, moves, moves,
+            pltpu.VMEM((SLOTS * 8, domains * 8), BF16), pltpu.VMEM((SLOTS * 3, domains * 8), BF16),
+            pltpu.VMEM((SLOTS * 3, BLOCK), BF16),
             pltpu.VMEM((SLOTS, 8, BLOCK), F32),
             pltpu.VMEM((SLOTS, KEEP, BLOCK), BF16),
             pltpu.VMEM((SLOTS + EXPORTS * FAR, BLOCK, BLOCK), BF16),

time: 51 us -> 50.9 us (level)
  no operation moved by 1% of the time
where the time goes in v4:
time: 50.9 us; the launch traced here: 50.7 us
  Pallas kernels  48.5 us (95%)
  other arithmetic  1.49 us (3%)
  between operations  0.64 us (1%)
    pallas_call x1, Pallas kernels, on_device(): pl.pallas_call(functools.partial(kernel, domains, bits), out_shape=(jax.S...  48.5 us
    add x1, other arithmetic, on_device(): return (new_pos + TIMESTEP * vel_out, vel_out)  1.49 us

profile of v4, /device:TPU:1, one launch (start us, length us, event | category | flops | bytes accessed | tf_op | source)
XLA Modules:
  0.0 50.7 jit_solution(5089273065503530661)
XLA Ops:
  0.6 48.5 %shard_map.86 = (f32[3,32,128]{2,1,0:T(8,128)}, f32[3,32,128]{2,1,0:T(8,128)}, f32[3,32,128]{2,1,0:T(8,128)}) custom-call(f32[3,32,128]{2,1,0:T(8,128)} %bitcast.10, f32[32,128]{1,0:T(8,128)} %mass_in.1, f32[3,32,128]{2,1,0:T(8,128)} %bitcast.11, s32[32]{0:T(128)} %dest.1, s32[4,32]{1,0:T(4,128)} %bitcast.12, s32[4,5]{1,0:T(4,128)} %bitcast.13, s32[4,20]{1,0:T(4,128)} %bitcast.14), custom_call_target="tpu_custom_call" | custom-call | tf_op jit(solution)/shard_map/pallas_call | solution.py:312
  49.2 1.5 %bitcast_add_fusion = (f32[32,3,128]{2,0,1:T(8,128)}, f32[32,3,128]{2,0,1:T(8,128)}) fusion(f32[3,32,128]{2,1,0:T(8,128)} %get-tuple-element.5, f32[3,32,128]{2,1,0:T(8,128)} %get-tuple-element.6, f32[3,32,128]{2,1,0:T(8,128)} %get-tuple-element.7), kind=kLoop, calls=%fused_computation | loop fusion | flops 49152 | bytes 245760 | tf_op jit(solution)/shard_map/add | solution.py:342

commit v5 on v4

--- a/solution.py
+++ b/solution.py
@@ -164,7 +164,7 @@
         count = lax.broadcasted_iota(jnp.int32, (rows, domains * 8), 1).astype(F32)
         return jnp.where(count == key, 1.0, 0.0).astype(BF16)
 
-    for copy in loads:
+    for copy in loads[:2]:
         copy.wait()
     pack_p[...] = packed(jnp.concatenate([pos[0], pos[1], pos[2], mass[...]], axis=0), 4.0)
     pl.semaphore_wait(barrier, domains - 1 + len(outer))
@@ -186,6 +186,7 @@
         )
 
     move(pack_p, land_p, 0, 8)
+    loads[2].wait()
     pack_v[...] = packed(
         jnp.concatenate([vel[0], vel[1], vel[2], jnp.zeros((SLOTS, BLOCK), F32)], axis=0), 3.0
     )

time: 50.9 us -> 50.9 us (level)
  no operation moved by 1% of the time
where the time goes in v5:
time: 50.9 us; the launch traced here: 50.7 us
  Pallas kernels  48.5 us (95%)
  other arithmetic  1.49 us (3%)
  between operations  0.64 us (1%)
    pallas_call x1, Pallas kernels, on_device(): pl.pallas_call(functools.partial(kernel, domains, bits), out_shape=(jax.S...  48.5 us
    add x1, other arithmetic, on_device(): return (new_pos + TIMESTEP * vel_out, vel_out)  1.49 us

profile of v5, /device:TPU:1, one launch (start us, length us, event | category | flops | bytes accessed | tf_op | source)
XLA Modules:
  0.0 50.7 jit_solution(16029220526694886077)
XLA Ops:
  0.6 48.5 %shard_map.86 = (f32[3,32,128]{2,1,0:T(8,128)}, f32[3,32,128]{2,1,0:T(8,128)}, f32[3,32,128]{2,1,0:T(8,128)}) custom-call(f32[3,32,128]{2,1,0:T(8,128)} %bitcast.10, f32[32,128]{1,0:T(8,128)} %mass_in.1, f32[3,32,128]{2,1,0:T(8,128)} %bitcast.11, s32[32]{0:T(128)} %dest.1, s32[4,32]{1,0:T(4,128)} %bitcast.12, s32[4,5]{1,0:T(4,128)} %bitcast.13, s32[4,20]{1,0:T(4,128)} %bitcast.14), custom_call_target="tpu_custom_call" | custom-call | tf_op jit(solution)/shard_map/pallas_call | solution.py:313
  49.2 1.5 %bitcast_add_fusion = (f32[32,3,128]{2,0,1:T(8,128)}, f32[32,3,128]{2,0,1:T(8,128)}) fusion(f32[3,32,128]{2,1,0:T(8,128)} %get-tuple-element.5, f32[3,32,128]{2,1,0:T(8,128)} %get-tuple-element.6, f32[3,32,128]{2,1,0:T(8,128)} %get-tuple-element.7), kind=kLoop, calls=%fused_computation | loop fusion | flops 49152 | bytes 245760 | tf_op jit(solution)/shard_map/add | solution.py:343
